TPU v7x, 256 devices: a whole 4x4x8 slice. The times are simulated.
256 devices in a mesh: slab: 8 (over y, core), seq: 32 (over z, x).
Axes of the slice: x: 4, y: 4, z: 8, core: 2. Of those that a mesh axis runs over, the one named last changes fastest.
Arguments:
- noise: float32 [2, 16, 2048], P(None, None, 'seq'), may hold values from -6 to 6
- plan: int32 [32], replicated, may hold values from 1 to 1000, as said below
- slides: int32 [2], replicated, may hold values from 7 to 9
- w_in: bfloat16 [16, 1152], replicated, may hold values from -1.5 to 1.5
- w_mod: bfloat16 [256, 2304], replicated, may hold values from -0.375 to 0.375
- w_qkv: bfloat16 [1152, 3456], replicated, may hold values from -0.088388348 to 0.088388348
- qk_gain: float32 [2, 1152], replicated, may hold values from 0.5 to 6
- w_o: bfloat16 [1152, 1152], replicated, may hold values from -0.1875 to 0.1875
- w_out: bfloat16 [1152, 16], replicated, may hold values from -0.1875 to 0.1875
Outputs:
- trajectory: float32 [16, 2, 16, 2048], P('slab', None, None, 'seq')
- anchor: float32 [2, 16, 2048], P(None, None, 'seq')
Inputs may be any that keep to these rules, and one draw needn't show every extreme that they name: `plan`: strictly decreasing; the first entry is 1000.
All inputs are finite; a program needn't handle non-finite values.
Results may differ from a plain program's by a relative error of at most 0.0028.
Values may be sent and summed in bfloat16 or wider, within the bound.
A program may use at most 128 MiB of HBM per device.

v0:
```python
import math

import jax
import jax.numpy as jnp
from jax import lax
from jax.sharding import PartitionSpec as P

HEADS = 16
HD = 72
STEPS_DEV = 2
SWEEPS = 2


norm_eps = 1e-06


def carried_in(shard, axis, combine, identity):
    devices, place = (lax.axis_size(axis), lax.axis_index(axis))
    everything = lax.all_gather(shard, axis)
    start = jnp.broadcast_to(jnp.asarray(identity, shard.dtype), shard.shape)

    def lap(k, before):
        reached = k < place
        new = combine(before, everything[k])
        return jnp.where(reached, new, before)

    return lax.fori_loop(0, devices, lap, start)


def layer_norm(tensor):
    average = jnp.mean(tensor, axis=-1, keepdims=True)
    centered = tensor - average
    spread = jnp.mean(centered * centered, axis=-1, keepdims=True)
    return centered * lax.rsqrt(spread + norm_eps)


def time_features(levels, feature_count):
    half_width = feature_count // 2
    frequency = jnp.exp(-math.log(10000.0) * jnp.arange(half_width, dtype=jnp.float32) / half_width)
    angles = levels[:, None] * frequency[None, :]
    return jnp.concatenate([jnp.cos(angles), jnp.sin(angles)], axis=-1)


def head_norm(tensor, gain_row):
    inv_rms = lax.rsqrt(jnp.mean(tensor * tensor, axis=-1, keepdims=True) + norm_eps)
    return tensor * inv_rms * gain_row.reshape(HEADS, HD)


def project_in(states, levels, w_in, w_mod, w_qkv, qk_gain):
    model_width = w_in.shape[1]
    embedded = jnp.einsum(
        "scpt,pd->sctd", states.astype(jnp.bfloat16), w_in, preferred_element_type=jnp.float32
    )
    features = time_features(levels, w_mod.shape[0]).astype(jnp.bfloat16)
    modulation = jnp.dot(features, w_mod, preferred_element_type=jnp.float32)
    normed = (
        layer_norm(embedded) * (1.0 + modulation[:, None, None, :model_width])
        + modulation[:, None, None, model_width:]
    )
    joined = jnp.einsum(
        "sctd,de->scte", normed.astype(jnp.bfloat16), w_qkv, preferred_element_type=jnp.float32
    )
    step_count, clip_count, row_count = joined.shape[:3]
    split_shape = (step_count, clip_count, row_count, HEADS, HD)
    queries = head_norm(joined[..., :model_width].reshape(split_shape), qk_gain[0]).astype(
        jnp.bfloat16
    )
    key_part = head_norm(
        joined[..., model_width : 2 * model_width].reshape(split_shape), qk_gain[1]
    ).astype(jnp.bfloat16)
    value_part = joined[..., 2 * model_width :].reshape(split_shape).astype(jnp.bfloat16)
    packed = jnp.concatenate([queries, key_part, value_part], axis=-1)
    packed = packed.transpose(0, 1, 3, 2, 4).reshape(
        step_count, clip_count * HEADS, row_count, 3 * HD
    )
    return (packed, embedded)


def attend(packed):
    items, pairs, count = packed.shape[:3]
    queries = packed[..., :HD]
    key_part = packed[..., HD : 2 * HD]
    value_part = packed[..., 2 * HD :]
    block_rows = 512
    blocked = jnp.moveaxis(queries.reshape(items, pairs, count // block_rows, block_rows, HD), 2, 0)

    def one_block(query_block):
        scores = jnp.einsum(
            "ipqh,ipkh->ipqk", query_block, key_part, preferred_element_type=jnp.float32
        ) * HD ** (-0.5)
        row_max = jnp.max(scores, axis=-1, keepdims=True)
        lifted = jnp.exp(scores - row_max)
        row_total = jnp.sum(lifted, axis=-1, keepdims=True)
        weights_bf = (lifted / row_total).astype(jnp.bfloat16)
        return jnp.einsum(
            "ipqk,ipkh->ipqh", weights_bf, value_part, preferred_element_type=jnp.float32
        ).astype(jnp.bfloat16)

    result = lax.map(one_block, blocked)
    return jnp.moveaxis(result, 0, 2).reshape(items, pairs, count, HD)


def project_out(returned, embedded, w_o, w_out):
    step_count, clip_count, row_count, model_width = embedded.shape
    merged = returned.reshape(step_count, clip_count, HEADS, row_count, HD).transpose(0, 1, 3, 2, 4)
    merged = merged.reshape(step_count, clip_count, row_count, model_width)
    mixed = embedded + jnp.einsum("sctd,de->scte", merged, w_o, preferred_element_type=jnp.float32)
    return jnp.einsum(
        "sctd,dp->scpt",
        layer_norm(mixed).astype(jnp.bfloat16),
        w_out,
        preferred_element_type=jnp.float32,
    )


def add_terms(earlier, later):
    return earlier + later


def on_device(noise, plan, slides, w_in, w_mod, w_qkv, qk_gain, w_o, w_out):
    slab_rank = lax.axis_index("slab")
    per_device = STEPS_DEV
    anchor_state = noise
    states = jnp.broadcast_to(anchor_state[None], (per_device,) + anchor_state.shape)
    offset = jnp.zeros((), jnp.int32)
    for sweep_index in range(SWEEPS):
        first_step = offset + slab_rank * per_device
        levels = lax.dynamic_slice_in_dim(plan, first_step, per_device + 1).astype(jnp.float32)
        step_size = (levels[1:] - levels[:-1]) / 1000.0
        packed, embedded = project_in(states, levels[:-1], w_in, w_mod, w_qkv, qk_gain)
        attended = attend(lax.all_to_all(packed, "seq", split_axis=1, concat_axis=2, tiled=True))
        returned = lax.all_to_all(attended, "seq", split_axis=2, concat_axis=1, tiled=True)
        velocity = project_out(returned, embedded, w_o, w_out)
        terms = step_size[:, None, None, None] * velocity
        own_sum = jnp.sum(terms, axis=0)
        within = jnp.concatenate(
            [jnp.zeros_like(terms[:1]), jnp.cumsum(terms[:-1], axis=0)], axis=0
        )
        prefix = carried_in(own_sum, "slab", add_terms, jnp.zeros_like(own_sum))
        drift_sum = lax.psum(own_sum, "slab")
        states = anchor_state[None] + prefix[None] + within
        final_state = anchor_state + drift_sum
        shift_by = slides[sweep_index]
        gathered = lax.all_gather(states, "slab", axis=0, tiled=True)
        extended = jnp.concatenate(
            [gathered, jnp.broadcast_to(final_state[None], gathered.shape)], axis=0
        )
        states = lax.dynamic_slice_in_dim(extended, slab_rank * per_device + shift_by, per_device)
        anchor_state = lax.dynamic_index_in_dim(extended, shift_by, 0, keepdims=False)
        offset = offset + shift_by
    return (states, anchor_state)


def solution(mesh):
    return jax.shard_map(
        on_device,
        mesh=mesh,
        in_specs=(P(None, None, "seq"), P(), P(), P(), P(), P(), P(), P(), P()),
        out_specs=(P("slab", None, None, "seq"), P(None, None, "seq")),
        check_vma=False,
    )
```

profile of v0, /device:TPU:1, one launch (start us, length us, event | category | flops | bytes accessed | tf_op | source)
XLA Modules:
  0.0 505.0 jit_solution(12852359041702564795)
XLA Ops:
  7.9 6.1 %fusion.66 = f32[2,2,64,3456]{3,2,1,0:T(8,128)S(1)} fusion(bf16[1152,3456]{1,0:T(8,128)(2,1)} %param.22, f32[2,2,64,1152]{3,2,1,0:T(8,128)S(1)} %get-tuple-element.353, f32[2,1152]{1,0:T(2,128)S(1)} %get-tuple-element.335, f32[2,1152]{1,0:T(2,128)S(1)} %get-tuple-element.334, f32[2,2,64]{2,1,0:T(2,128)S(1)} %add_rsqrt_fusion.7, ...), kind=kOutput, calls=%fused_computation.48 | convolution fusion | flops 2039906304 | bytes 12701696 | tf_op jit(solution)/shard_map/sctd,de->scte/dot_general | solution.py:60
  38.6 12.4 %all-to-all-start = ((bf16[2,32,64,216]{3,2,0,1:T(8,128)(2,1)}), bf16[2,32,64,216]{3,2,0,1:T(8,128)(2,1)}, u32[]{:S(2)}, u32[]{:S(2)}) async-start(bf16[2,32,64,216]{3,2,0,1:T(8,128)(2,1)} %copy.62), calls=%async_computation | async-start | bytes 4194304 | tf_op jit(solution)/shard_map/all_to_all | solution.py:131
  51.0 48.4 %all-to-all-done = bf16[2,32,64,216]{3,2,0,1:T(8,128)(2,1)} async-done(((bf16[2,32,64,216]{3,2,0,1:T(8,128)(2,1)}), bf16[2,32,64,216]{3,2,0,1:T(8,128)(2,1)}, u32[]{:S(2)}, u32[]{:S(2)}) %all-to-all-start) | async-done | bytes 1769504 | tf_op jit(solution)/shard_map/all_to_all | solution.py:131
  110.2 48.0 %while.48 = (s32[]{:T(128)}, bf16[4,2,1,512,72]{3,4,1,2,0:T(8,128)(2,1)S(1)}, bf16[4,2,1,512,72]{3,4,1,2,0:T(8,128)(2,1)}, bf16[2,1,2048,72]{2,3,0,1:T(8,128)(2,1)}, bf16[2,1,2048,72]{2,3,0,1:T(8,128)(2,1)}, /*index=5*/s32[]{:T(128)}) while((s32[]{:T(128)}, bf16[4,2,1,512,72]{3,4,1,2,0:T(8,128)(2,1)S(1)}, ...), condition=%wide.region_7.8_spmd, body=%wide.region_4.7_spmd.sunk | while | flops 614541312 | bytes 18260552 | solution.py:99
  110.2 7.1 %fusion.171 = (f32[2,512]{1,0:T(2,128)S(1)}, f32[2,512,2048]{2,1,0:T(8,128)}) fusion(bf16[2,1,2048,72]{2,3,0,1:T(8,128)(2,1)} %get-tuple-element.501, bf16[4,2,1,512,72]{3,4,1,2,0:T(8,128)(2,1)} %get-tuple-element.500, s32[]{:T(128)} %get-tuple-element.492), kind=kOutput, calls=%fused_computation.167.clone.1 | convolution fusion | flops 308283392 | bytes 9130496 | tf_op jit(solution)/shard_map/while/body/eval_jaxpr/sub | solution.py:92
  122.2 7.1 %fusion.171 = (f32[2,512]{1,0:T(2,128)S(1)}, f32[2,512,2048]{2,1,0:T(8,128)}) fusion(bf16[2,1,2048,72]{2,3,0,1:T(8,128)(2,1)} %get-tuple-element.501, bf16[4,2,1,512,72]{3,4,1,2,0:T(8,128)(2,1)} %get-tuple-element.500, s32[]{:T(128)} %get-tuple-element.492), kind=kOutput, calls=%fused_computation.167.clone.1 | convolution fusion | flops 308283392 | bytes 9130496 | tf_op jit(solution)/shard_map/while/body/eval_jaxpr/sub | solution.py:92
  134.2 7.1 %fusion.171 = (f32[2,512]{1,0:T(2,128)S(1)}, f32[2,512,2048]{2,1,0:T(8,128)}) fusion(bf16[2,1,2048,72]{2,3,0,1:T(8,128)(2,1)} %get-tuple-element.501, bf16[4,2,1,512,72]{3,4,1,2,0:T(8,128)(2,1)} %get-tuple-element.500, s32[]{:T(128)} %get-tuple-element.492), kind=kOutput, calls=%fused_computation.167.clone.1 | convolution fusion | flops 308283392 | bytes 9130496 | tf_op jit(solution)/shard_map/while/body/eval_jaxpr/sub | solution.py:92
  146.2 7.1 %fusion.171 = (f32[2,512]{1,0:T(2,128)S(1)}, f32[2,512,2048]{2,1,0:T(8,128)}) fusion(bf16[2,1,2048,72]{2,3,0,1:T(8,128)(2,1)} %get-tuple-element.501, bf16[4,2,1,512,72]{3,4,1,2,0:T(8,128)(2,1)} %get-tuple-element.500, s32[]{:T(128)} %get-tuple-element.492), kind=kOutput, calls=%fused_computation.167.clone.1 | convolution fusion | flops 308283392 | bytes 9130496 | tf_op jit(solution)/shard_map/while/body/eval_jaxpr/sub | solution.py:92
  160.2 6.7 %all-to-all-start.1 = ((bf16[2,1,2048,72]{3,0,1,2:T(2,128)(2,1)}), bf16[2,1,2048,72]{3,0,1,2:T(2,128)(2,1)}, u32[]{:S(2)}, u32[]{:S(2)}) async-start(bf16[2,1,2048,72]{3,0,1,2:T(2,128)(2,1)} %bitcast.195), calls=%async_computation.1 | async-start | bytes 2097152 | tf_op jit(solution)/shard_map/all_to_all | solution.py:132
  169.1 23.2 %all-to-all-done.1 = bf16[2,1,2048,72]{3,0,1,2:T(2,128)(2,1)} async-done(((bf16[2,1,2048,72]{3,0,1,2:T(2,128)(2,1)}), bf16[2,1,2048,72]{3,0,1,2:T(2,128)(2,1)}, u32[]{:S(2)}, u32[]{:S(2)}) %all-to-all-start.1) | async-done | bytes 589856 | tf_op jit(solution)/shard_map/all_to_all | solution.py:132
  200.6 16.8 %all-gather = f32[16,16,64]{2,1,0:T(8,128)S(1)} all-gather(f32[2,16,64]{2,1,0:T(8,128)S(1)} %get-tuple-element.356), channel_id=2, replica_groups=mesh['slab'=8,'seq'=32] {'slab'}, dimensions={0}, use_global_device_ids=true | all-gather | bytes 73728 | tf_op jit(solution)/shard_map/all_gather | solution.py:19
  217.4 22.6 %psum.14 = f32[2,16,64]{2,1,0:T(8,128)S(1)} all-reduce(f32[2,16,64]{2,1,0:T(8,128)S(1)} %get-tuple-element.356), channel_id=1, replica_groups=mesh['slab'=8,'seq'=32] {'slab'}, use_global_device_ids=true, to_apply=%region_13.14 | all-reduce | flops 2048 | bytes 16384 | tf_op jit(solution)/shard_map/psum | solution.py:140
  240.3 16.4 %all_gather.20 = f32[16,2,16,64]{3,2,1,0:T(8,128)S(1)} all-gather(f32[2,2,16,64]{3,2,1,0:T(8,128)S(1)} %pad_add_fusion.1), channel_id=1, replica_groups=mesh['slab'=8,'seq'=32] {'slab'}, dimensions={0}, use_global_device_ids=true | all-gather | bytes 147456 | tf_op jit(solution)/shard_map/all_gather | solution.py:144
  300.3 48.4 %all-to-all-done.2 = bf16[2,32,64,216]{3,2,0,1:T(8,128)(2,1)} async-done(((bf16[2,32,64,216]{3,2,0,1:T(8,128)(2,1)}), bf16[2,32,64,216]{3,2,0,1:T(8,128)(2,1)}, u32[]{:S(2)}, u32[]{:S(2)}) %all-to-all-start.2) | async-done | bytes 1769504 | tf_op jit(solution)/shard_map/all_to_all | solution.py:131
  359.3 48.0 %while.49 = (s32[]{:T(128)}, bf16[4,2,1,512,72]{3,4,1,2,0:T(8,128)(2,1)S(1)}, bf16[4,2,1,512,72]{3,4,1,2,0:T(8,128)(2,1)}, bf16[2,1,2048,72]{2,3,0,1:T(8,128)(2,1)}, bf16[2,1,2048,72]{2,3,0,1:T(8,128)(2,1)}, /*index=5*/s32[]{:T(128)}) while((s32[]{:T(128)}, bf16[4,2,1,512,72]{3,4,1,2,0:T(8,128)(2,1)S(1)}, ...), condition=%wide.region_21.22_spmd, body=%wide.region_18.21_spmd.sunk | while | flops 614541312 | bytes 18260552 | solution.py:99
  359.3 7.1 %fusion.176 = (f32[2,512]{1,0:T(2,128)S(1)}, f32[2,512,2048]{2,1,0:T(8,128)}) fusion(bf16[2,1,2048,72]{2,3,0,1:T(8,128)(2,1)} %get-tuple-element.537, bf16[4,2,1,512,72]{3,4,1,2,0:T(8,128)(2,1)} %get-tuple-element.536, s32[]{:T(128)} %get-tuple-element.528), kind=kOutput, calls=%fused_computation.168.clone.1 | convolution fusion | flops 308283392 | bytes 9130496 | tf_op jit(solution)/shard_map/while/body/eval_jaxpr/sub | solution.py:92
  371.3 7.1 %fusion.176 = (f32[2,512]{1,0:T(2,128)S(1)}, f32[2,512,2048]{2,1,0:T(8,128)}) fusion(bf16[2,1,2048,72]{2,3,0,1:T(8,128)(2,1)} %get-tuple-element.537, bf16[4,2,1,512,72]{3,4,1,2,0:T(8,128)(2,1)} %get-tuple-element.536, s32[]{:T(128)} %get-tuple-element.528), kind=kOutput, calls=%fused_computation.168.clone.1 | convolution fusion | flops 308283392 | bytes 9130496 | tf_op jit(solution)/shard_map/while/body/eval_jaxpr/sub | solution.py:92
  383.3 7.1 %fusion.176 = (f32[2,512]{1,0:T(2,128)S(1)}, f32[2,512,2048]{2,1,0:T(8,128)}) fusion(bf16[2,1,2048,72]{2,3,0,1:T(8,128)(2,1)} %get-tuple-element.537, bf16[4,2,1,512,72]{3,4,1,2,0:T(8,128)(2,1)} %get-tuple-element.536, s32[]{:T(128)} %get-tuple-element.528), kind=kOutput, calls=%fused_computation.168.clone.1 | convolution fusion | flops 308283392 | bytes 9130496 | tf_op jit(solution)/shard_map/while/body/eval_jaxpr/sub | solution.py:92
  395.3 7.1 %fusion.176 = (f32[2,512]{1,0:T(2,128)S(1)}, f32[2,512,2048]{2,1,0:T(8,128)}) fusion(bf16[2,1,2048,72]{2,3,0,1:T(8,128)(2,1)} %get-tuple-element.537, bf16[4,2,1,512,72]{3,4,1,2,0:T(8,128)(2,1)} %get-tuple-element.536, s32[]{:T(128)} %get-tuple-element.528), kind=kOutput, calls=%fused_computation.168.clone.1 | convolution fusion | flops 308283392 | bytes 9130496 | tf_op jit(solution)/shard_map/while/body/eval_jaxpr/sub | solution.py:92
  409.3 7.4 %all-to-all-start.3 = ((bf16[2,1,2048,72]{3,0,1,2:T(2,128)(2,1)}), bf16[2,1,2048,72]{3,0,1,2:T(2,128)(2,1)}, u32[]{:S(2)}, u32[]{:S(2)}) async-start(bf16[2,1,2048,72]{3,0,1,2:T(2,128)(2,1)} %bitcast.194), calls=%async_computation.3 | async-start | bytes 2097152 | tf_op jit(solution)/shard_map/all_to_all | solution.py:132
  421.0 21.5 %all-to-all-done.3 = bf16[2,1,2048,72]{3,0,1,2:T(2,128)(2,1)} async-done(((bf16[2,1,2048,72]{3,0,1,2:T(2,128)(2,1)}), bf16[2,1,2048,72]{3,0,1,2:T(2,128)(2,1)}, u32[]{:S(2)}, u32[]{:S(2)}) %all-to-all-start.3) | async-done | bytes 589856 | tf_op jit(solution)/shard_map/all_to_all | solution.py:132
  450.8 15.8 %all-gather.1 = f32[16,16,64]{2,1,0:T(8,128)S(1)} all-gather(f32[2,16,64]{2,1,0:T(8,128)S(1)} %get-tuple-element.362), channel_id=3, replica_groups=mesh['slab'=8,'seq'=32] {'slab'}, dimensions={0}, use_global_device_ids=true | all-gather | bytes 73728 | tf_op jit(solution)/shard_map/all_gather | solution.py:19
  466.6 20.4 %psum.15 = f32[2,16,64]{2,1,0:T(8,128)S(1)} all-reduce(f32[2,16,64]{2,1,0:T(8,128)S(1)} %get-tuple-element.362), channel_id=1, replica_groups=mesh['slab'=8,'seq'=32] {'slab'}, use_global_device_ids=true, to_apply=%region_27.28 | all-reduce | flops 2048 | bytes 16384 | tf_op jit(solution)/shard_map/psum | solution.py:140
  487.3 16.2 %all_gather.23 = f32[16,2,16,64]{3,2,1,0:T(8,128)S(1)} all-gather(f32[2,2,16,64]{3,2,1,0:T(8,128)S(1)} %pad_add_fusion), channel_id=1, replica_groups=mesh['slab'=8,'seq'=32] {'slab'}, dimensions={0}, use_global_device_ids=true | all-gather | bytes 147456 | tf_op jit(solution)/shard_map/all_gather | solution.py:144
  (156 shorter events, 159.9 us)
Async XLA Ops:
  0.6 196.8 %copy-start = (bf16[1152,1152]{1,0:T(8,128)(2,1)S(1)}, bf16[1152,1152]{1,0:T(8,128)(2,1)}, u32[]{:S(2)}) copy-start(bf16[1152,1152]{1,0:T(8,128)(2,1)} %param.24) | copy-start | bytes 7962628
  7.7 6.4 %copy-start.4 = (f32[2,2,64,1152]{3,2,1,0:T(8,128)}, f32[2,2,64,1152]{3,2,1,0:T(8,128)S(1)}, u32[]{:S(2)}) copy-start(f32[2,2,64,1152]{3,2,1,0:T(8,128)S(1)} %get-tuple-element.353) | copy-start | bytes 3538948
  15.7 6.2 %copy-start.13 = (f32[2,1152]{1,0:T(2,128)S(1)}, f32[2,1152]{1,0:T(2,128)}, u32[]{:S(2)}) copy-start(f32[2,1152]{1,0:T(2,128)} %param.23) | copy-start | bytes 27652
  31.0 1.9 copy-start.1
  32.9 1.6 copy-start.2
  38.6 60.9 %all-to-all-start = ((bf16[2,32,64,216]{3,2,0,1:T(8,128)(2,1)}), bf16[2,32,64,216]{3,2,0,1:T(8,128)(2,1)}, u32[]{:S(2)}, u32[]{:S(2)}) async-start(bf16[2,32,64,216]{3,2,0,1:T(8,128)(2,1)} %copy.62), calls=%async_computation | async-start | bytes 4194304 | tf_op jit(solution)/shard_map/all_to_all | solution.py:131
  160.2 32.1 %all-to-all-start.1 = ((bf16[2,1,2048,72]{3,0,1,2:T(2,128)(2,1)}), bf16[2,1,2048,72]{3,0,1,2:T(2,128)(2,1)}, u32[]{:S(2)}, u32[]{:S(2)}) async-start(bf16[2,1,2048,72]{3,0,1,2:T(2,128)(2,1)} %bitcast.195), calls=%async_computation.1 | async-start | bytes 2097152 | tf_op jit(solution)/shard_map/all_to_all | solution.py:132
  197.4 2.7 copy-start.10
  199.8 40.4 %copy-start.12 = (f32[2,16,64]{2,1,0:T(8,128)S(1)}, f32[2,16,64]{2,1,0:T(8,128)}, u32[]{:S(2)}) copy-start(f32[2,16,64]{2,1,0:T(8,128)} %param.17) | copy-start | bytes 24580
  199.8 57.6 %copy-start.9 = (bf16[16,1152]{1,0:T(8,128)(2,1)S(1)}, bf16[16,1152]{1,0:T(8,128)(2,1)}, u32[]{:S(2)}) copy-start(bf16[16,1152]{1,0:T(8,128)(2,1)} %param.20) | copy-start | bytes 110596
  217.4 40.8 %copy-start.14 = (f32[2,1152]{1,0:T(2,128)S(1)}, f32[2,1152]{1,0:T(2,128)}, u32[]{:S(2)}) copy-start(f32[2,1152]{1,0:T(2,128)} %get-tuple-element.332) | copy-start | bytes 27652
  217.4 40.8 %copy-start.15 = (f32[2,1152]{1,0:T(2,128)S(1)}, f32[2,1152]{1,0:T(2,128)}, u32[]{:S(2)}) copy-start(f32[2,1152]{1,0:T(2,128)} %get-tuple-element.333) | copy-start | bytes 27652
  256.7 0.7 copy-start.7
  257.8 6.4 %copy-start.3 = (f32[2,2,64,1152]{3,2,1,0:T(8,128)}, f32[2,2,64,1152]{3,2,1,0:T(8,128)S(1)}, u32[]{:S(2)}) copy-start(f32[2,2,64,1152]{3,2,1,0:T(8,128)S(1)} %get-tuple-element.359) | copy-start | bytes 3538948
  290.0 1.7 copy-start.5
  290.0 1.9 copy-start.6
  294.6 54.0 %all-to-all-start.2 = ((bf16[2,32,64,216]{3,2,0,1:T(8,128)(2,1)}), bf16[2,32,64,216]{3,2,0,1:T(8,128)(2,1)}, u32[]{:S(2)}, u32[]{:S(2)}) async-start(bf16[2,32,64,216]{3,2,0,1:T(8,128)(2,1)} %copy.76), calls=%async_computation.2 | async-start | bytes 4194304 | tf_op jit(solution)/shard_map/all_to_all | solution.py:131
  409.3 33.1 %all-to-all-start.3 = ((bf16[2,1,2048,72]{3,0,1,2:T(2,128)(2,1)}), bf16[2,1,2048,72]{3,0,1,2:T(2,128)(2,1)}, u32[]{:S(2)}, u32[]{:S(2)}) async-start(bf16[2,1,2048,72]{3,0,1,2:T(2,128)(2,1)} %bitcast.194), calls=%async_computation.3 | async-start | bytes 2097152 | tf_op jit(solution)/shard_map/all_to_all | solution.py:132
  447.6 2.7 copy-start.11
  447.6 2.7 copy-start.16
  450.0 37.3 %copy-start.8 = (f32[16,2,16,64]{3,2,1,0:T(8,128)S(1)}, f32[16,2,16,64]{3,2,1,0:T(8,128)}, u32[]{:S(2)}) copy-start(f32[16,2,16,64]{3,2,1,0:T(8,128)} %copy-done.7) | copy-start | bytes 393220
where the time goes:
time: 515 us; the launch traced here: 505 us
  waiting for transfers between devices  141 us (27%)
  matrix products  118 us (23%)
  blocking collectives  108 us (21%)
  local copies, waits for them, and re-layouts  71.4 us (14%)
  starting transfers between devices  32.2 us (6%)
  other arithmetic  26.6 us (5%)
  between operations  6.25 us (1%)
    all_to_all x2, waiting for transfers between devices, on_device(): lax.all_to_all(packed, 'seq', split_axis=1, concat_axis=2, tiled=True)  96.8 us
    sub x8, matrix products, one_block(): lifted = jnp.exp(scores - row_max)  56.6 us
    all_to_all x2, waiting for transfers between devices, on_device(): lax.all_to_all(attended, 'seq', split_axis=2, concat_axis=1, tiled=True)  44.6 us
    psum x2, blocking collectives, on_device(): drift_sum = lax.psum(own_sum, 'slab')  43 us
    dot_general x8, matrix products, one_block(): jnp.einsum('ipqk,ipkh->ipqh', weights_bf, value_part, preferred_element_t...  39.3 us
    all_gather x2, blocking collectives, on_device(): gathered = lax.all_gather(states, 'slab', axis=0, tiled=True)  32.6 us
    all_gather x2, blocking collectives, carried_in(): everything = lax.all_gather(shard, axis)  32.6 us
    all_to_all x2, starting transfers between devices, on_device(): lax.all_to_all(packed, 'seq', split_axis=1, concat_axis=2, tiled=True)  18.1 us
  transfers between devices with their start and end apart: 4, of which 4 were waited for; matrix products, arithmetic and copies ran while one was open for 0% of the time, Pallas kernels for 0%

commit v1 on v0

v1 whole, which is shorter than its diff:
```python
import functools
import math

import jax
import jax.numpy as jnp
import numpy as np
from jax import lax
from jax.experimental import pallas as pl
from jax.experimental.pallas import tpu as pltpu
from jax.sharding import PartitionSpec as P

HEADS = 16
HD = 72
STEPS_DEV = 2
SWEEPS = 2
PATCH = 16
FE = 24
LANES = 128
WIDTH = HEADS * HD
GROUPS = 4
WINDOW_LANES = 384

norm_eps = 1e-06
MESH = pl.DeviceIdType.MESH
f32 = jnp.float32
bf16 = jnp.bfloat16


def dot(a, b):
    return lax.dot_general(a, b, (((1,), (0,)), ((), ())), preferred_element_type=f32)


def dot_nt(a, b):
    return lax.dot_general(a, b, (((1,), (1,)), ((), ())), preferred_element_type=f32)


def split(x):
    high = x.astype(bf16)
    return high, (x - high.astype(f32)).astype(bf16)


def fold_kernel(m_ref, gain_ref, at_ref, bk_ref, bq_ref, mv_ref):
    lane = lax.broadcasted_iota(jnp.int32, (FE, LANES), 1)

    def three(x):
        high = x.astype(bf16).astype(f32)
        col = lax.broadcasted_iota(jnp.int32, x.shape, 1)
        return jnp.where((col >= FE) & (col < 2 * FE), x - high, high).astype(bf16)

    pad = jnp.zeros((LANES - 3 * FE, WINDOW_LANES), f32)
    for g in range(GROUPS):
        start = 256 * g
        mq = m_ref[0, :, start : start + WINDOW_LANES]
        mk = m_ref[0, :, WIDTH + start : WIDTH + start + WINDOW_LANES]
        mv = m_ref[0, :, 2 * WIDTH + start : 2 * WIDTH + start + WINDOW_LANES]
        gain = gain_ref[:, start : start + WINDOW_LANES]
        col = lax.broadcasted_iota(jnp.int32, (FE, WINDOW_LANES), 1) + start

        def block(x, rows_per_head):
            parts = []
            for p in range(4):
                h = 4 * g + p
                parts.append(jnp.where((col >= HD * h) & (col < HD * (h + 1)), x, 0.0))
                if rows_per_head > FE:
                    parts.append(jnp.zeros((rows_per_head - FE, WINDOW_LANES), f32))
            return jnp.concatenate(parts, axis=0)

        def product(left, right):
            lh, ll = split(block(left, FE))
            rh, rl = split(jnp.concatenate([right, right, right, pad], axis=0))
            out = dot_nt(
                jnp.concatenate([lh, ll], axis=0), jnp.concatenate([rh, rl], axis=0)
            )
            rows = 4 * FE
            return out[:rows, :LANES] + out[rows:, :LANES] + out[:rows, LANES:]

        rows = pl.ds(4 * FE * g, 4 * FE)
        bk_ref[0, rows, :] = three(product(mk, mk * (1.0 / HD)))
        bq_ref[0, rows, :] = three(product(mq, mq * (1.0 / HD)))
        a = three(product(mk * gain, mq)).astype(f32)
        for p in range(4):
            piece = a[FE * p : FE * (p + 1)]
            full = jnp.concatenate(
                [piece, piece, piece, jnp.zeros((LANES - 3 * FE, LANES), f32)], axis=0
            )
            at_ref[0, pl.ds(LANES * (4 * g + p), LANES), :] = full.astype(bf16)
        left = block(mv, 32)
        cols = []
        if start:
            cols.append(jnp.zeros((LANES, start), f32))
        cols.append(left)
        if start + WINDOW_LANES < WIDTH:
            cols.append(jnp.zeros((LANES, WIDTH - start - WINDOW_LANES), f32))
        mv_ref[0, pl.ds(LANES * g, LANES), :] = jnp.concatenate(cols, axis=1).astype(bf16)


def fold(m, gain):
    combos = m.shape[0]

    def spec(rows, cols):
        return pl.BlockSpec((1, rows, cols), lambda t: (t, 0, 0))

    return pl.pallas_call(
        fold_kernel,
        grid=(combos,),
        in_specs=[spec(FE, 3 * WIDTH), pl.BlockSpec((1, WIDTH), lambda t: (0, 0))],
        out_specs=[
            spec(HEADS * LANES, LANES),
            spec(HEADS * FE, LANES),
            spec(HEADS * FE, LANES),
            spec(HEADS * 32, WIDTH),
        ],
        out_shape=[
            jax.ShapeDtypeStruct((combos, HEADS * LANES, LANES), bf16),
            jax.ShapeDtypeStruct((combos, HEADS * FE, LANES), bf16),
            jax.ShapeDtypeStruct((combos, HEADS * FE, LANES), bf16),
            jax.ShapeDtypeStruct((combos, HEADS * 32, WIDTH), bf16),
        ],
        compiler_params=pltpu.CompilerParams(vmem_limit_bytes=32 << 20),
    )(m, gain)


def time_features(levels, feature_count):
    half_width = feature_count // 2
    frequency = jnp.exp(-math.log(10000.0) * jnp.arange(half_width, dtype=f32) / half_width)
    angles = levels[:, None] * frequency[None, :]
    return jnp.concatenate([jnp.cos(angles), jnp.sin(angles)], axis=-1)


def prepare(levels, w_in, w_mod, w_qkv, qk_gain):
    combos = levels.shape[0]
    features = time_features(levels, w_mod.shape[0]).astype(bf16)
    modulation = jnp.dot(features, w_mod, preferred_element_type=f32)
    wide = w_in.astype(f32)
    centered = wide - jnp.mean(wide, axis=1, keepdims=True)
    gram = lax.dot_general(
        centered, centered, (((1,), (1,)), ((), ())), precision=lax.Precision.HIGHEST
    ) * (1.0 / WIDTH)
    g1 = gram.astype(bf16)
    rest = gram - g1.astype(f32)
    g2 = rest.astype(bf16)
    g3 = (rest - g2.astype(f32)).astype(bf16)
    gram3 = jnp.concatenate([g1, g2, g3], axis=0)
    rows = jnp.concatenate(
        [
            centered[None] * (1.0 + modulation[:, None, :WIDTH]),
            modulation[:, None, WIDTH:],
            jnp.zeros((combos, FE - PATCH - 1, WIDTH), f32),
        ],
        axis=1,
    ).reshape(combos * FE, WIDTH)
    high, low = split(rows)
    both = jnp.dot(jnp.concatenate([high, low], axis=0), w_qkv, preferred_element_type=f32)
    m = (both[: combos * FE] + both[combos * FE :]).reshape(combos, FE, 3 * WIDTH)
    gain = (qk_gain[0] * qk_gain[1] * (HD**-0.5 * math.log2(math.e))).reshape(1, WIDTH)
    return gram3, fold(m, gain)


def features_of(x, gram):
    g = dot(gram, x.astype(bf16))
    t = g[:PATCH] + g[PATCH : 2 * PATCH] + g[2 * PATCH :]
    spread = jnp.sum(x * t, axis=0, keepdims=True)
    u = x * lax.rsqrt(jnp.maximum(spread, 0.0) + norm_eps)
    count = x.shape[1]
    first = lax.broadcasted_iota(jnp.int32, (FE - PATCH, count), 0) == 0
    u = jnp.concatenate([u, jnp.where(first, 1.0, 0.0)], axis=0)
    high = u.astype(bf16).astype(f32)
    low = u - high
    f = jnp.concatenate([high, high, low, jnp.zeros((LANES - 3 * FE, count), f32)], axis=0)
    return u, f.astype(bf16)


def head_scale(weights, u, f):
    t = dot(weights, f).reshape(HEADS, FE, f.shape[1])
    total = jnp.sum(t * u[None], axis=1)
    return lax.rsqrt(jnp.maximum(total, 0.0) + norm_eps)


def attend_kernel(
    step_ref, own_ref, all_ref, gram_ref, at_ref, bk_ref, bq_ref, mv_ref, wo_ref, win_ref,
    wout_ref, out_ref, xs, kf, rho, qs, scores, zs, att,
):
    sources, kinds = all_ref.shape[:2]
    tokens = sources * 64
    gram = gram_ref[...]
    chunk = 512
    lane = lax.broadcasted_iota(jnp.int32, (PATCH, LANES), 1)

    for s in range(STEPS_DEV):
        k = s % kinds
        if s < kinds:
            for p in range(sources // 2):
                a = all_ref[2 * p, k].astype(f32)
                b = all_ref[2 * p + 1, k].astype(f32)
                xs[:, pl.ds(LANES * p, LANES)] = jnp.where(lane < 64, a, pltpu.roll(b, 64, 1))
                xs[:, pl.ds(tokens + LANES * p, LANES)] = jnp.where(
                    lane < 64, pltpu.roll(a, 64, 1), b
                )

        @pl.loop(0, 2 * tokens // chunk)
        def _(n):
            cols = pl.ds(pl.multiple_of(n * chunk, chunk), chunk)
            u, f = features_of(xs[:, cols], gram)
            kf[:, cols] = f
            scale = head_scale(bk_ref[s], u, f)
            for g in range(GROUPS):
                rho[g, pl.ds(0, 4), cols] = scale[4 * g : 4 * g + 4]

        own = own_ref[k].astype(f32)
        u, f = features_of(own, gram)
        scale = head_scale(bq_ref[s], u, f)
        row = lax.broadcasted_iota(jnp.int32, (LANES, LANES), 0)
        for h in range(HEADS):
            q = dot(at_ref[s, pl.ds(LANES * h, LANES), :], f) * scale[h : h + 1]
            high = q.astype(bf16).astype(f32)
            q = jnp.where((row >= FE) & (row < 2 * FE), q - high, high).T
            for c in range(2):
                qs[c, pl.ds(64 * h, 64), :] = q[64 * c : 64 * (c + 1)].astype(bf16)

        lane64 = lax.broadcasted_iota(jnp.int32, (64, LANES), 1)
        for c in range(2):
            keys = pl.ds(tokens * c, tokens)

            @pl.loop(0, GROUPS)
            def _(g):
                sc = dot(qs[c, pl.ds(pl.multiple_of(g * 256, 256), 256), :], kf[:, keys])
                r = rho[g, pl.ds(0, 4), keys]
                sc = sc.reshape(4, 64, tokens) * r[:, None, :]
                sc = sc.reshape(256, tokens)
                top = jnp.max(sc, axis=1, keepdims=True)
                probs = jnp.exp2(sc - top).astype(bf16)
                o = dot_nt(probs, kf[:, keys])
                o = o + pltpu.roll(o, LANES - 2 * FE, 1)
                z = jnp.zeros((64, LANES), f32)
                for p in range(4):
                    piece = o[64 * p : 64 * (p + 1)]
                    piece = jnp.where(lane64 < FE, piece / piece[:, PATCH : PATCH + 1], 0.0)
                    z = z + (pltpu.roll(piece, 32 * p, 1) if p else piece)
                zs[g, pl.ds(64 * c, 64), :] = z.astype(bf16)

        z = jnp.concatenate([zs[g] for g in range(GROUPS)], axis=1)
        att[pl.ds(LANES * s, LANES), :] = dot(z, mv_ref[s]).astype(bf16)

    for s in range(STEPS_DEV):
        k = s % kinds
        embedded = lax.dot_general(
            own_ref[k], win_ref[...], (((0,), (0,)), ((), ())), preferred_element_type=f32
        )
        mixed = embedded + dot(att[pl.ds(LANES * s, LANES), :], wo_ref[...])
        centered = mixed - jnp.mean(mixed, axis=1, keepdims=True)
        spread = jnp.mean(centered * centered, axis=1, keepdims=True)
        normed = (centered * lax.rsqrt(spread + norm_eps)).astype(bf16)
        out_ref[s] = dot_nt(wout_ref[...], normed) * step_ref[s]


def attend(step_size, own, everything, gram3, weights, w_o, w_in, w_out_t):
    at, bk, bq, mv = weights
    sources = everything.shape[0]
    tokens = sources * 64
    vmem = pl.BlockSpec(memory_space=pltpu.VMEM)
    return pl.pallas_call(
        attend_kernel,
        in_specs=[pl.BlockSpec(memory_space=pltpu.SMEM)] + [vmem] * 10,
        out_specs=vmem,
        out_shape=jax.ShapeDtypeStruct((STEPS_DEV, PATCH, LANES), f32),
        scratch_shapes=[
            pltpu.VMEM((PATCH, 2 * tokens), f32),
            pltpu.VMEM((LANES, 2 * tokens), bf16),
            pltpu.VMEM((GROUPS, 8, 2 * tokens), f32),
            pltpu.VMEM((2, HEADS * 64, LANES), bf16),
            pltpu.VMEM((256, tokens), f32),
            pltpu.VMEM((GROUPS, LANES, LANES), bf16),
            pltpu.VMEM((2 * LANES, WIDTH), bf16),
        ],
        compiler_params=pltpu.CompilerParams(vmem_limit_bytes=48 << 20),
    )(step_size, own, everything, gram3, at, bk, bq, mv, w_o, w_in, w_out_t)


def greet(axes):
    barrier = pltpu.get_barrier_semaphore()
    total = 0
    for axis, count in axes:
        me = lax.axis_index(axis)

        @pl.loop(1, count)
        def _(i):
            pl.semaphore_signal(
                barrier, inc=1, device_id={axis: lax.rem(me + i, count)}, device_id_type=MESH
            )

        total += count - 1
    pl.semaphore_wait(barrier, total)


def spread_to(axis, count, src, dst, send, recv, local):
    me = lax.axis_index(axis)

    def copy(i, place):
        return pltpu.make_async_remote_copy(
            src_ref=src,
            dst_ref=dst.at[place],
            send_sem=send.at[i],
            recv_sem=recv.at[i],
            device_id={axis: lax.rem(me + i, count)},
            device_id_type=MESH,
        )

    @pl.loop(1, count)
    def _(i):
        copy(i, me).start()

    here = pltpu.make_async_copy(src, dst.at[me], local)
    here.start()
    here.wait()

    @pl.loop(1, count)
    def _(i):
        copy(i, lax.rem(me + count - i, count)).wait()


def gather_kernel(count, x_ref, out_ref, send, recv, local):
    greet((("seq", count),))
    spread_to("seq", count, x_ref, out_ref, send, recv, local)


def gather(x, count):
    vmem = pl.BlockSpec(memory_space=pltpu.VMEM)
    return pl.pallas_call(
        functools.partial(gather_kernel, count),
        in_specs=[vmem],
        out_specs=vmem,
        out_shape=jax.ShapeDtypeStruct((count,) + x.shape, x.dtype),
        scratch_shapes=[
            pltpu.SemaphoreType.DMA((count,)),
            pltpu.SemaphoreType.DMA((count,)),
            pltpu.SemaphoreType.DMA,
        ],
        compiler_params=pltpu.CompilerParams(collective_id=1, has_side_effects=True),
    )(x)


def picard(first, shift, anchor, terms_ref, slabs):
    steps = STEPS_DEV * slabs
    state = [anchor] * (STEPS_DEV + 1)
    limits = [first + a for a in range(STEPS_DEV)] + [shift]
    for j in range(steps):
        term = terms_ref[j // STEPS_DEV, j % STEPS_DEV]
        state = [v + jnp.where(j < n, term, 0.0) for v, n in zip(state, limits)]
    return state


def slide_kernel(
    slabs, count, shift_ref, terms_ref, anchor_ref, own_ref, new_anchor_ref, all_ref,
    every, send_a, recv_a, send_b, recv_b, local,
):
    greet((("slab", slabs), ("seq", count)))
    spread_to("slab", slabs, terms_ref, every, send_a, recv_a, local.at[0])
    shift = shift_ref[0]
    first = STEPS_DEV * lax.axis_index("slab") + shift
    state = picard(first, shift, anchor_ref[...], every, slabs)
    for a in range(STEPS_DEV):
        own_ref[a] = state[a].astype(bf16)
    new_anchor_ref[...] = state[-1]
    spread_to("seq", count, own_ref, all_ref, send_b, recv_b, local.at[1])


def slide(shift, terms, anchor, slabs, count):
    vmem = pl.BlockSpec(memory_space=pltpu.VMEM)
    return pl.pallas_call(
        functools.partial(slide_kernel, slabs, count),
        in_specs=[pl.BlockSpec(memory_space=pltpu.SMEM), vmem, vmem],
        out_specs=[vmem] * 3,
        out_shape=[
            jax.ShapeDtypeStruct(terms.shape, bf16),
            jax.ShapeDtypeStruct(anchor.shape, f32),
            jax.ShapeDtypeStruct((count,) + terms.shape, bf16),
        ],
        scratch_shapes=[
            pltpu.VMEM((slabs,) + terms.shape, f32),
            pltpu.SemaphoreType.DMA((slabs,)),
            pltpu.SemaphoreType.DMA((slabs,)),
            pltpu.SemaphoreType.DMA((count,)),
            pltpu.SemaphoreType.DMA((count,)),
            pltpu.SemaphoreType.DMA((2,)),
        ],
        compiler_params=pltpu.CompilerParams(collective_id=2, has_side_effects=True),
    )(shift, terms, anchor)


def finish_kernel(slabs, shift_ref, terms_ref, anchor_ref, out_ref, new_anchor_ref, every, send, recv, local):
    greet((("slab", slabs),))
    spread_to("slab", slabs, terms_ref, every, send, recv, local)
    shift = shift_ref[0]
    first = STEPS_DEV * lax.axis_index("slab") + shift
    state = picard(first, shift, anchor_ref[...], every, slabs)
    for a in range(STEPS_DEV):
        out_ref[a] = state[a]
    new_anchor_ref[...] = state[-1]


def finish(shift, terms, anchor, slabs):
    vmem = pl.BlockSpec(memory_space=pltpu.VMEM)
    return pl.pallas_call(
        functools.partial(finish_kernel, slabs),
        in_specs=[pl.BlockSpec(memory_space=pltpu.SMEM), vmem, vmem],
        out_specs=[vmem] * 2,
        out_shape=[
            jax.ShapeDtypeStruct(terms.shape, f32),
            jax.ShapeDtypeStruct(anchor.shape, f32),
        ],
        scratch_shapes=[
            pltpu.VMEM((slabs,) + terms.shape, f32),
            pltpu.SemaphoreType.DMA((slabs,)),
            pltpu.SemaphoreType.DMA((slabs,)),
            pltpu.SemaphoreType.DMA,
        ],
        compiler_params=pltpu.CompilerParams(collective_id=3, has_side_effects=True),
    )(shift, terms, anchor)


def on_device(noise, plan, slides, w_in, w_mod, w_qkv, qk_gain, w_o, w_out):
    slabs, count = lax.axis_size("slab"), lax.axis_size("seq")
    anchor = jnp.concatenate([noise[0], noise[1]], axis=-1)
    own = anchor.astype(bf16)[None]
    everything = gather(own, count)
    first = STEPS_DEV * lax.axis_index("slab")
    levels, sizes = [], []
    for offset in (jnp.zeros((), jnp.int32), slides[0]):
        part = lax.dynamic_slice_in_dim(plan, offset + first, STEPS_DEV + 1).astype(f32)
        levels.append(part[:-1])
        sizes.append((part[1:] - part[:-1]) / 1000.0)
    gram3, weights = prepare(jnp.concatenate(levels), w_in, w_mod, w_qkv, qk_gain)
    w_out_t = w_out.T
    for sweep in range(SWEEPS):
        mine = [w[STEPS_DEV * sweep : STEPS_DEV * (sweep + 1)] for w in weights]
        terms = attend(sizes[sweep], own, everything, gram3, mine, w_o, w_in, w_out_t)
        shift = slides[sweep : sweep + 1]
        if sweep + 1 < SWEEPS:
            own, anchor, everything = slide(shift, terms, anchor, slabs, count)
        else:
            states, anchor = finish(shift, terms, anchor, slabs)
    half = LANES // 2
    states = jnp.stack([states[..., :half], states[..., half:]], axis=1)
    anchor = jnp.stack([anchor[..., :half], anchor[..., half:]], axis=0)
    return (states, anchor)


def solution(mesh):
    return jax.shard_map(
        on_device,
        mesh=mesh,
        in_specs=(P(None, None, "seq"), P(), P(), P(), P(), P(), P(), P(), P()),
        out_specs=(P("slab", None, None, "seq"), P(None, None, "seq")),
        check_vma=False,
    )
```

time: 515 us -> 167 us (0.32); the launches traced: 505 us -> 166 us
  waiting for transfers between devices: 141 us -> 0 us
  Pallas kernels: 0 us -> 125 us
  matrix products: 118 us -> 5.76 us
  blocking collectives: 108 us -> 0 us
  local copies, waits for them, and re-layouts: 71.4 us -> 26.7 us
  starting transfers between devices: 32.2 us -> 0 us
  other arithmetic: 26.6 us -> 6.31 us
    all_to_all x4 -> x0, waiting for transfers between devices: 141 us -> none  [the longest x2 96.8 us: on_device(): lax.all_to_all(packed, 'seq', split_axis=1, concat_axis=2, tiled=True)]
    pallas_call x0 -> x6, Pallas kernels: none -> 125 us  [the longest x2 72.6 us: attend(): pl.pallas_call(attend_kernel, in_specs=[pl.BlockSpec(memory_space=pltpu.S...]
    all_gather x4 -> x0, blocking collectives: 65.2 us -> none  [the longest x2 32.6 us: on_device(): gathered = lax.all_gather(states, 'slab', axis=0, tiled=True)]
    sub x8 -> x0, matrix products: 56.6 us -> none  [one_block(): lifted = jnp.exp(scores - row_max)]
    dot_general x18 -> x3, matrix products: 61.8 us -> 5.76 us  [the longest x1 5.2 us: prepare(): jnp.dot(jnp.concatenate([high, low], axis=0), w_qkv, preferred_element_ty...]
    psum x2 -> x0, blocking collectives: 43 us -> none  [on_device(): drift_sum = lax.psum(own_sum, 'slab')]
    all_to_all x4 -> x0, starting transfers between devices: 32.2 us -> none  [the longest x2 18.1 us: on_device(): lax.all_to_all(packed, 'seq', split_axis=1, concat_axis=2, tiled=True)]
    reshape x12 -> x0, local copies, waits for them, and re-layouts: 31.1 us -> none  [the longest x2 7.64 us: project_in(): joined[..., :model_width].reshape(split_shape)]
  transfers between devices with their start and end apart: 4 -> 0, of which waited for: 4 -> 0; matrix products, arithmetic and copies ran while one was open for 0% -> 0% of each run, Pallas kernels for 0% -> 0%
where the time goes in v1:
time: 167 us; the launch traced here: 166 us
  Pallas kernels  125 us (75%)
  local copies, waits for them, and re-layouts  26.7 us (16%)
  other arithmetic  6.31 us (4%)
  matrix products  5.76 us (3%)
    pallas_call x2, Pallas kernels, attend(): pl.pallas_call(attend_kernel, in_specs=[pl.BlockSpec(memory_space=pltpu.S...  72.6 us
    pallas_call x1, Pallas kernels, slide(): pl.pallas_call(functools.partial(slide_kernel, slabs, count), in_specs=[p...  23.2 us
    unnamed x45, local copies, waits for them, and re-layouts  17.2 us
    pallas_call x1, Pallas kernels, gather(): pl.pallas_call(functools.partial(gather_kernel, count), in_specs=[vmem],...  16.5 us
    pallas_call x1, Pallas kernels, finish(): pl.pallas_call(functools.partial(finish_kernel, slabs), in_specs=[pl.Bloc...  8.66 us
    dot_general x1, matrix products, prepare(): jnp.dot(jnp.concatenate([high, low], axis=0), w_qkv, preferred_element_ty...  5.2 us
    slice x4, local copies, waits for them, and re-layouts, on_device(): mine = [w[STEPS_DEV * sweep:STEPS_DEV * (sweep + 1)] for w in weights]  4.83 us
    pallas_call x1, Pallas kernels, fold(): pl.pallas_call(fold_kernel, grid=(combos,), in_specs=[spec(FE, 3 * WIDTH)...  4.32 us

profile of v1, /device:TPU:1, one launch (start us, length us, event | category | flops | bytes accessed | tf_op | source)
XLA Modules:
  0.0 165.5 jit_solution(17702306837465249312)
XLA Ops:
  0.7 1.4 fusion.22
  2.6 0.8 dynamic-slice_convert_fusion
  4.5 0.9 convert_reduce_fusion
  5.4 0.8 convert_subtract_fusion
  6.6 5.2 %fusion = f32[192,3456]{1,0:T(8,128)S(1)} fusion(bf16[1152,3456]{1,0:T(8,128)(2,1)} %param.14, bf16[96,1152]{1,0:T(8,128)(2,1)S(1)} %get-tuple-element.24, bf16[96,1152]{1,0:T(8,128)(2,1)S(1)} %get-tuple-element.25), kind=kOutput, calls=%fused_computation.3 | convolution fusion | flops 1529708544 | bytes 11059200 | tf_op jit(solution)/shard_map/dot_general | solution.py:153
  12.5 4.3 %shard_map.105 = (bf16[4,2048,128]{2,1,0:T(8,128)(2,1)S(1)}, bf16[4,384,128]{2,1,0:T(8,128)(2,1)S(1)}, bf16[4,384,128]{2,1,0:T(8,128)(2,1)S(1)}, bf16[4,512,1152]{2,1,0:T(8,128)(2,1)S(1)}) custom-call(f32[4,24,3456]{2,1,0:T(8,128)S(1)} %bitcast.25, f32[1,1152]{1,0:T(1,128)S(1)} %multiply_multiply_fusion.gain_ref), custom_call_target="tpu_custom_call" | custom-call | tf_op jit(solution)/shard_map/pallas_call | solution.py:103
  16.8 1.8 %fusion.14 = (bf16[2,512,1152]{2,1,0:T(8,128)(2,1)S(1)}, bf16[2,512,1152]{2,1,0:T(8,128)(2,1)}) fusion(bf16[4,512,1152]{2,1,0:T(8,128)(2,1)S(1)} %get-tuple-element.14), kind=kLoop, calls=%fused_computation.49 | loop fusion | bytes 9437184 | tf_op jit(solution)/shard_map/slice | solution.py:435
  18.6 1.5 fusion.15
  24.8 16.5 %shard_map.104.all_ref = bf16[32,1,16,128]{3,2,1,0:T(8,128)(2,1)} custom-call(bf16[1,16,128]{2,1,0:T(8,128)(2,1)} %pad_maximum_fusion.3.x_ref.own_ref), custom_call_target="tpu_custom_call" | custom-call | tf_op jit(solution)/shard_map/pallas_call | solution.py:328
  41.3 1.7 %copy-done.1 = bf16[2,512,1152]{2,1,0:T(8,128)(2,1)S(1)} copy-done((bf16[2,512,1152]{2,1,0:T(8,128)(2,1)S(1)}, bf16[2,512,1152]{2,1,0:T(8,128)(2,1)}, u32[]{:S(2)}) %copy-start.1) | copy-done | bytes 2359320
  43.0 1.2 copy-done.3
  44.2 0.9 copy-done.6
  45.1 0.9 copy-done.7
  46.8 0.9 copy-done.11
  49.8 36.2 %shard_map.106.terms_ref = f32[2,16,128]{2,1,0:T(8,128)S(1)} custom-call(f32[2]{0:T(128)S(1)} %copy-done.19, bf16[1,16,128]{2,1,0:T(8,128)(2,1)S(1)} %copy-done.17, bf16[32,1,16,128]{3,2,1,0:T(8,128)(2,1)S(1)} %copy-done.11, bf16[48,16]{1,0:T(8,128)(2,1)S(1)} %copy.15.gram_ref, bf16[2,2048,128]{2,1,0:T(8,128)(2,1)S(1)} %copy-done.3, ...), custom_call_target="tpu_custom_call" | custom-call | tf_op jit(solution)/shard_map/pallas_call | solution.py:261
  87.3 23.2 %shard_map.107 = (bf16[2,16,128]{2,1,0:T(8,128)(2,1)}, f32[16,128]{1,0:T(8,128)}, bf16[32,2,16,128]{3,2,1,0:T(8,128)(2,1)}) custom-call(s32[1]{0:T(128)} %get-tuple-element.55.shift_ref, f32[2,16,128]{2,1,0:T(8,128)} %copy-done.15, f32[16,128]{1,0:T(8,128)} %pad_maximum_fusion.2.anchor_ref), custom_call_target="tpu_custom_call" | custom-call | tf_op jit(solution)/shard_map/pallas_call | solution.py:369
  110.6 1.2 copy-done.2
  111.8 0.9 copy-done.4
  112.7 0.9 copy-done.5
  114.4 0.9 copy-done.12
  116.9 36.4 %shard_map.108.terms_ref = f32[2,16,128]{2,1,0:T(8,128)S(1)} custom-call(f32[2]{0:T(128)S(1)} %get-tuple-element.57.step_ref, bf16[2,16,128]{2,1,0:T(8,128)(2,1)S(1)} %copy-done.18, bf16[32,2,16,128]{3,2,1,0:T(8,128)(2,1)S(1)} %copy-done.12, bf16[48,16]{1,0:T(8,128)(2,1)S(1)} %copy.15.gram_ref, bf16[2,2048,128]{2,1,0:T(8,128)(2,1)S(1)} %copy-done.2, ...), custom_call_target="tpu_custom_call" | custom-call | tf_op jit(solution)/shard_map/pallas_call | solution.py:261
  153.9 8.7 %shard_map.109 = (f32[2,16,128]{2,1,0:T(8,128)}, f32[16,128]{1,0:T(8,128)}) custom-call(s32[1]{0:T(128)} %get-tuple-element.56.shift_ref, f32[2,16,128]{2,1,0:T(8,128)} %copy-done.16, f32[16,128]{1,0:T(8,128)} %get-tuple-element.17.anchor_ref), custom_call_target="tpu_custom_call" | custom-call | tf_op jit(solution)/shard_map/pallas_call | solution.py:403
  162.6 0.8 slice_bitcast_fusion.4
  164.1 0.9 slice_bitcast_fusion.2
  (62 shorter events, 15.0 us)
Async XLA Ops:
  0.6 3.6 %copy-start = (bf16[256,2304]{1,0:T(8,128)(2,1)S(1)}, bf16[256,2304]{1,0:T(8,128)(2,1)}, u32[]{:S(2)}) copy-start(bf16[256,2304]{1,0:T(8,128)(2,1)} %param.13) | copy-start | bytes 3538948
  11.8 0.7 copy-start.21
  18.6 3.1 %copy-start.8 = (bf16[16,1152]{1,0:T(8,128)(2,1)S(1)}, bf16[16,1152]{1,0:T(8,128)(2,1)}, u32[]{:S(2)}) copy-start(bf16[16,1152]{1,0:T(8,128)(2,1)} %win_ref.3) | copy-start | bytes 110596
  41.3 1.7 %copy-start.1 = (bf16[2,512,1152]{2,1,0:T(8,128)(2,1)S(1)}, bf16[2,512,1152]{2,1,0:T(8,128)(2,1)}, u32[]{:S(2)}) copy-start(bf16[2,512,1152]{2,1,0:T(8,128)(2,1)} %get-tuple-element.27.mv_ref) | copy-start | bytes 7077892
  43.0 1.2 copy-start.3
  44.2 0.9 copy-start.6
  45.1 0.9 copy-start.7
  46.0 0.8 copy-start.9
  46.8 0.9 copy-start.11
  47.7 0.8 copy-start.13
  48.5 0.7 copy-start.17
  49.2 0.7 copy-start.19
  49.8 36.9 %copy-start.20 = (f32[2,16,64]{2,1,0:T(8,128)S(1)}, f32[2,16,64]{2,1,0:T(8,128)}, u32[]{:S(2)}) copy-start(f32[2,16,64]{2,1,0:T(8,128)} %param.9) | copy-start | bytes 24580
  86.0 0.6 copy-start.15
  110.6 1.2 copy-start.2
  111.8 0.9 copy-start.4
  112.7 0.9 copy-start.5
  113.7 0.8 copy-start.10
  114.4 0.9 copy-start.12
  115.4 0.8 copy-start.14
  116.2 0.7 copy-start.18
  153.3 0.6 copy-start.16

commit v2 on v0

v2 whole, which is shorter than its diff:
```python
import math

import jax
import jax.numpy as jnp
import numpy as np
from jax import lax
from jax.experimental import pallas as pl
from jax.experimental.pallas import tpu as pltpu
from jax.sharding import PartitionSpec as P

HEADS = 16
HD = 72
STEPS_DEV = 2
SWEEPS = 2
COMBOS = STEPS_DEV * SWEEPS
CLIPS = 2
PATCH = 16
FREQ = 256
FE = 24
LANES = 128
OWN = 64
WIDTH = HEADS * HD
GROUPS = 4
WINDOW_LANES = 384
HB = 8
ROWS = HB * OWN
SUB = 16
CHUNK = 1024

norm_eps = 1e-06
MESH = pl.DeviceIdType.MESH
f32 = jnp.float32
bf16 = jnp.bfloat16


def dot(a, b):
    return lax.dot_general(a, b, (((1,), (0,)), ((), ())), preferred_element_type=f32)


def dot_nt(a, b):
    return lax.dot_general(a, b, (((1,), (1,)), ((), ())), preferred_element_type=f32)


def split(x):
    high = x.astype(bf16)
    return high, (x - high.astype(f32)).astype(bf16)


def modulated_rows(plan_ref, slides_ref, freq_ref, w_mod, w_in, gram, lhs):
    first = STEPS_DEV * lax.axis_index("slab")
    row = lax.broadcasted_iota(jnp.int32, (8, FREQ // 2), 0)
    level = jnp.zeros((8, FREQ // 2), f32)
    for t in range(COMBOS):
        place = first + t % STEPS_DEV
        if t >= STEPS_DEV:
            place = place + slides_ref[0]
        level = jnp.where(row == t, plan_ref[place].astype(f32), level)
    angles = level * freq_ref[...]
    features = jnp.concatenate([jnp.cos(angles), jnp.sin(angles)], axis=1).astype(bf16)
    modulation = dot(features, w_mod[...])
    wide = w_in[...].astype(f32)
    centered = wide - jnp.mean(wide, axis=1, keepdims=True)
    square = lax.dot_general(
        centered, centered, (((1,), (1,)), ((), ())),
        precision=lax.Precision.HIGHEST, preferred_element_type=f32,
    ) * (1.0 / WIDTH)
    g1 = square.astype(bf16)
    rest = square - g1.astype(f32)
    g2 = rest.astype(bf16)
    g3 = (rest - g2.astype(f32)).astype(bf16)
    for n, g in enumerate((g1, g2, g3)):
        gram[pl.ds(PATCH * n, PATCH), :] = g
    under = lax.broadcasted_iota(jnp.int32, (FE - PATCH, WIDTH), 0)
    rows = []
    for t in range(COMBOS):
        rows.append(centered * (1.0 + modulation[t : t + 1, :WIDTH]))
        rows.append(jnp.where(under == 0, modulation[t : t + 1, WIDTH:], 0.0))
    high, low = split(jnp.concatenate(rows, axis=0))
    lhs[pl.ds(0, COMBOS * FE), :] = high
    lhs[pl.ds(COMBOS * FE, COMBOS * FE), :] = low


def project(lhs, w_part, m_ref, part):
    @pl.loop(0, WIDTH // WINDOW_LANES)
    def _(n):
        at = pl.multiple_of(n * WINDOW_LANES, WINDOW_LANES)
        both = dot(lhs[...], w_part[:, pl.ds(at, WINDOW_LANES)])
        both = both[: COMBOS * FE] + both[COMBOS * FE :]
        to = pl.ds(pl.multiple_of(part * WIDTH + at, LANES), WINDOW_LANES)
        for t in range(COMBOS):
            m_ref[t, :, to] = both[FE * t : FE * (t + 1)]


def fold(t, m_ref, gain_ref, at_ref, bk_ref, bq_ref, mv_ref):
    def three(x):
        high = x.astype(bf16).astype(f32)
        col = lax.broadcasted_iota(jnp.int32, x.shape, 1)
        return jnp.where((col >= FE) & (col < 2 * FE), x - high, high).astype(bf16)

    pad = jnp.zeros((LANES - 3 * FE, WINDOW_LANES), f32)
    both_gains = gain_ref[0:1, :] * gain_ref[1:2, :] * (HD**-0.5 * math.log2(math.e))
    for g in range(GROUPS):
        start = 256 * g
        mq = m_ref[t, :, start : start + WINDOW_LANES]
        mk = m_ref[t, :, WIDTH + start : WIDTH + start + WINDOW_LANES]
        mv = m_ref[t, :, 2 * WIDTH + start : 2 * WIDTH + start + WINDOW_LANES]
        gain = both_gains[:, start : start + WINDOW_LANES]
        col = lax.broadcasted_iota(jnp.int32, (FE, WINDOW_LANES), 1) + start

        def block(x, rows_per_head):
            parts = []
            for p in range(4):
                h = 4 * g + p
                parts.append(jnp.where((col >= HD * h) & (col < HD * (h + 1)), x, 0.0))
                if rows_per_head > FE:
                    parts.append(jnp.zeros((rows_per_head - FE, WINDOW_LANES), f32))
            return jnp.concatenate(parts, axis=0)

        def product(left, right):
            lh, ll = split(block(left, FE))
            rh, rl = split(jnp.concatenate([right, right, right, pad], axis=0))
            out = dot_nt(
                jnp.concatenate([lh, ll], axis=0), jnp.concatenate([rh, rl], axis=0)
            )
            rows = 4 * FE
            return out[:rows, :LANES] + out[rows:, :LANES] + out[:rows, LANES:]

        rows = pl.ds(4 * FE * g, 4 * FE)
        bk_ref[t, rows, :] = three(product(mk, mk * (1.0 / HD)))
        bq_ref[t, rows, :] = three(product(mq, mq * (1.0 / HD)))
        a = three(product(mk * gain, mq)).astype(f32)
        for p in range(4):
            piece = a[FE * p : FE * (p + 1)]
            full = jnp.concatenate(
                [piece, piece, piece, jnp.zeros((LANES - 3 * FE, LANES), f32)], axis=0
            )
            at_ref[t, pl.ds(LANES * (4 * g + p), LANES), :] = full.astype(bf16)
        left = block(mv, 32)
        cols = []
        if start:
            cols.append(jnp.zeros((LANES, start), f32))
        cols.append(left)
        if start + WINDOW_LANES < WIDTH:
            cols.append(jnp.zeros((LANES, WIDTH - start - WINDOW_LANES), f32))
        mv_ref[t, pl.ds(LANES * g, LANES), :] = jnp.concatenate(cols, axis=1).astype(bf16)


def features_of(x, gram):
    g = dot(gram, x.astype(bf16))
    t = g[:PATCH] + g[PATCH : 2 * PATCH] + g[2 * PATCH :]
    spread = jnp.sum(x * t, axis=0, keepdims=True)
    u = x * lax.rsqrt(jnp.maximum(spread, 0.0) + norm_eps)
    count = x.shape[1]
    first = lax.broadcasted_iota(jnp.int32, (FE - PATCH, count), 0) == 0
    u = jnp.concatenate([u, jnp.where(first, 1.0, 0.0)], axis=0)
    high = u.astype(bf16).astype(f32)
    low = u - high
    f = jnp.concatenate([high, high, low, jnp.zeros((LANES - 3 * FE, count), f32)], axis=0)
    return u, f.astype(bf16)


def head_scale(weights, u, f):
    t = dot(weights, f).reshape(HEADS, FE, f.shape[1])
    total = jnp.sum(t * u[None], axis=1)
    return lax.rsqrt(jnp.maximum(total, 0.0) + norm_eps)


def own_queries(sweep, kinds, own_ref, gram, at_ref, bq_ref, qs):
    row = lax.broadcasted_iota(jnp.int32, (LANES, LANES), 0)
    for s in range(STEPS_DEV):
        t = STEPS_DEV * sweep + s
        if s < kinds:
            u, f = features_of(own_ref[s].astype(f32), gram)
        scale = head_scale(bq_ref[t], u, f)
        for h in range(HEADS):
            q = dot(at_ref[t, pl.ds(LANES * h, LANES), :], f) * scale[h : h + 1]
            high = q.astype(bf16).astype(f32)
            q = jnp.where((row >= FE) & (row < 2 * FE), q - high, high).T.astype(bf16)
            for c in range(CLIPS):
                lines = pl.ds(OWN * (h % HB), OWN)
                qs[CLIPS * s + c, h // HB, lines, :] = q[OWN * c : OWN * (c + 1)]


def all_keys(sweep, kinds, all_ref, gram, bk_ref, xs, kf, rho):
    sources = all_ref.shape[0]
    tokens = sources * OWN
    lane = lax.broadcasted_iota(jnp.int32, (PATCH, LANES), 1)
    for s in range(kinds):
        for p in range(sources // 2):
            a = all_ref[2 * p, s].astype(f32)
            b = all_ref[2 * p + 1, s].astype(f32)
            cols = pl.ds(LANES * p, LANES)
            xs[0, :, cols] = jnp.where(lane < OWN, a, pltpu.roll(b, OWN, 1))
            xs[1, :, cols] = jnp.where(lane < OWN, pltpu.roll(a, OWN, 1), b)

        @pl.loop(0, CLIPS)
        def _(c):
            for n in range(tokens // CHUNK):
                cols = pl.ds(n * CHUNK, CHUNK)
                u, f = features_of(xs[c, :, cols], gram)
                kf[CLIPS * s + c, :, cols] = f
                for v in range(s, STEPS_DEV, kinds):
                    scale = head_scale(bk_ref[STEPS_DEV * sweep + v], u, f)
                    for g in range(GROUPS):
                        rho[CLIPS * v + c, g, pl.ds(0, 4), cols] = scale[4 * g : 4 * g + 4]


def attend(kinds, tokens, qs, kf, rho, sc, pr, zs):
    lane = lax.broadcasted_iota(jnp.int32, (OWN, LANES), 1)
    parts = tokens // 256
    per = HEADS // HB
    blocks = CLIPS * STEPS_DEV * per

    def pair_of(block):
        pair = block // per
        return pair, pair % (CLIPS * kinds), block % per

    def stages(score, soft, value, slot):
        if score is not None:
            s_pair, s_keys, s_part = pair_of(score)
            q = qs[s_pair, s_part]
        if value is not None:
            v_pair, v_keys, v_part = pair_of(value)
            out = jnp.zeros((ROWS, LANES), f32)
        for n in range(parts):
            keys = pl.ds(256 * n, 256)
            if score is not None:
                t = dot(q, kf[s_keys, :, keys])
                for p in range(HB):
                    r = rho[s_pair, s_part * (HB // 4) + p // 4, pl.ds(p % 4, 1), keys]
                    sc[slot][pl.ds(OWN * p, OWN), keys] = t[OWN * p : OWN * (p + 1)] * r
            if soft is not None:
                some = ROWS // parts
                for m in range(some // SUB):
                    lines = pl.ds(some * n + SUB * m, SUB)
                    x = sc[1 - slot][lines, :]
                    x = x - jnp.max(x, axis=1, keepdims=True)
                    pr[1 - slot][lines, :] = jnp.exp2(x).astype(bf16)
            if value is not None:
                out = out + dot_nt(pr[slot][:, keys], kf[v_keys, :, keys])
        if value is not None:
            o = out + pltpu.roll(out, LANES - 2 * FE, 1)
            for g in range(HB // 4):
                z = jnp.zeros((OWN, LANES), f32)
                for p in range(4):
                    at = OWN * (4 * g + p)
                    piece = o[at : at + OWN]
                    piece = jnp.where(lane < FE, piece / piece[:, PATCH : PATCH + 1], 0.0)
                    z = z + (pltpu.roll(piece, 32 * p, 1) if p else piece)
                zs[v_pair, v_part * (HB // 4) + g] = z.astype(bf16)

    stages(0, None, None, 0)
    stages(1, 0, None, 1)

    @pl.loop(0, blocks // 2 - 1)
    def _(i):
        stages(2 * i + 2, 2 * i + 1, 2 * i, 0)
        stages(2 * i + 3, 2 * i + 2, 2 * i + 1, 1)

    stages(None, blocks - 1, blocks - 2, 0)
    stages(None, None, blocks - 1, 1)


def velocity_terms(sweep, kinds, sizes, own_ref, zs, mv_ref, w_o, w_in, w_out_t, out_ref):
    attended, embedded = [], []
    for s in range(STEPS_DEV):
        z = jnp.concatenate(
            [
                jnp.concatenate([zs[CLIPS * s + c, g] for g in range(GROUPS)], axis=1)
                for c in range(CLIPS)
            ],
            axis=0,
        )
        attended.append(dot(z, mv_ref[STEPS_DEV * sweep + s]).astype(bf16))
        embedded.append(
            lax.dot_general(
                own_ref[s % kinds], w_in[...], (((0,), (0,)), ((), ())),
                preferred_element_type=f32,
            )
        )
    mixed = jnp.concatenate(embedded, axis=0)
    mixed = mixed + dot(jnp.concatenate(attended, axis=0), w_o[...])
    centered = mixed - jnp.mean(mixed, axis=1, keepdims=True)
    spread = jnp.mean(centered * centered, axis=1, keepdims=True)
    normed = (centered * lax.rsqrt(spread + norm_eps)).astype(bf16)
    velocity = dot_nt(w_out_t[...], normed)
    for s in range(STEPS_DEV):
        out_ref[s] = velocity[:, LANES * s : LANES * (s + 1)] * sizes[s]


class Exchange:
    def __init__(self, axis, count, src, dst, send, recv):
        self.axis, self.count, self.src, self.dst = axis, count, src, dst
        self.send, self.recv = send, recv
        self.me = lax.axis_index(axis)

    def copy(self, i, place):
        return pltpu.make_async_remote_copy(
            src_ref=self.src,
            dst_ref=self.dst.at[place],
            send_sem=self.send.at[i],
            recv_sem=self.recv.at[i],
            device_id={self.axis: lax.rem(self.me + i, self.count)},
            device_id_type=MESH,
        )

    def start(self):
        @pl.loop(1, self.count)
        def _(i):
            self.copy(i, self.me).start()

        self.dst[self.me] = self.src[...]

    def wait(self):
        @pl.loop(1, self.count)
        def _(i):
            self.copy(i, lax.rem(self.me + self.count - i, self.count)).wait()


def greet(barrier, axis, count):
    me = lax.axis_index(axis)

    @pl.loop(1, count)
    def _(i):
        pl.semaphore_signal(
            barrier, inc=1, device_id={axis: lax.rem(me + i, count)}, device_id_type=MESH
        )


def picard(shift, anchor, terms_ref):
    slabs = terms_ref.shape[0]
    first = STEPS_DEV * lax.axis_index("slab") + shift
    limits = [first + a for a in range(STEPS_DEV)] + [shift]
    state = [anchor] * len(limits)
    for j in range(STEPS_DEV * slabs):
        term = terms_ref[j // STEPS_DEV, j % STEPS_DEV]
        state = [v + jnp.where(j < n, term, 0.0) for v, n in zip(state, limits)]
    return state


def window_kernel(
    plan_ref, slides_ref, freq_ref, noise_ref, w_in_hbm, w_mod_hbm, w_qkv_hbm, gain_hbm, w_o_hbm,
    w_out_hbm, states_ref, anchor_ref,
    noise, w_in, w_mod, wq, wk, wv, gain, w_o, w_out, load,
    lhs, m_ref, gram, at_ref, bk_ref, bq_ref, mv_ref, w_out_t,
    anchor, own0, own1, all0, all1, terms0, terms1, every0, every1,
    send0, recv0, send1, recv1, send2, recv2, send3, recv3,
    xs, kf, rho, qs, sc0, sc1, pr0, pr1, zs,
):
    slabs, count = every0.shape[0], all0.shape[0]
    tokens = count * OWN
    columns = [w_qkv_hbm.at[:, pl.ds(WIDTH * n, WIDTH)] for n in range(3)]
    pairs = (
        (noise_ref, noise), (w_in_hbm, w_in), (w_mod_hbm, w_mod), (columns[0], wq),
        (columns[1], wk), (columns[2], wv), (gain_hbm, gain), (w_out_hbm, w_out), (w_o_hbm, w_o),
    )
    loads = [pltpu.make_async_copy(a, b, load.at[n]) for n, (a, b) in enumerate(pairs)]
    for copy in loads:
        copy.start()
    barrier = pltpu.get_barrier_semaphore()
    greet(barrier, "seq", count)
    greet(barrier, "slab", slabs)

    loads[0].wait()
    start = jnp.concatenate([noise[0], noise[1]], axis=1)
    anchor[...] = start
    own0[0] = start.astype(bf16)
    loads[1].wait()
    loads[2].wait()
    modulated_rows(plan_ref, slides_ref, freq_ref, w_mod, w_in, gram, lhs)
    pl.semaphore_wait(barrier, count + slabs - 2)
    gather0 = Exchange("seq", count, own0, all0, send0, recv0)
    gather0.start()
    for n, part in enumerate((wq, wk, wv)):
        loads[3 + n].wait()
        project(lhs, part, m_ref, n)
    loads[6].wait()

    @pl.loop(0, COMBOS)
    def _(t):
        fold(t, m_ref, gain, at_ref, bk_ref, bq_ref, mv_ref)

    loads[7].wait()
    w_out_t[...] = w_out[...].astype(f32).T.astype(bf16)
    loads[8].wait()

    sc, pr = (sc0, sc1), (pr0, pr1)
    own, everyone = (own0, own1), (all0, all1)
    terms, every = (terms0, terms1), (every0, every1)
    sums = (
        Exchange("slab", slabs, terms0, every0, send1, recv1),
        Exchange("slab", slabs, terms1, every1, send3, recv3),
    )
    gather1 = Exchange("seq", count, own1, all1, send2, recv2)
    offset = 0
    for sweep in range(SWEEPS):
        kinds = own[sweep].shape[0]
        square = gram[...]
        own_queries(sweep, kinds, own[sweep], square, at_ref, bq_ref, qs)
        (gather0 if sweep == 0 else gather1).wait()
        all_keys(sweep, kinds, everyone[sweep], square, bk_ref, xs, kf, rho)
        attend(kinds, tokens, qs, kf, rho, sc, pr, zs)
        first = STEPS_DEV * lax.axis_index("slab") + offset
        levels = [plan_ref[first + a].astype(f32) for a in range(STEPS_DEV + 1)]
        sizes = [(levels[a + 1] - levels[a]) / 1000.0 for a in range(STEPS_DEV)]
        velocity_terms(
            sweep, kinds, sizes, own[sweep], zs, mv_ref, w_o, w_in, w_out_t, terms[sweep]
        )
        sums[sweep].start()
        sums[sweep].wait()
        shift = slides_ref[sweep]
        state = picard(shift, anchor[...], every[sweep])
        if sweep + 1 < SWEEPS:
            for a in range(STEPS_DEV):
                own1[a] = state[a].astype(bf16)
            gather1.start()
            anchor[...] = state[-1]
            offset = offset + shift
        else:
            for a in range(STEPS_DEV):
                for c in range(CLIPS):
                    states_ref[a, c] = state[a][:, OWN * c : OWN * (c + 1)]
            for c in range(CLIPS):
                anchor_ref[c] = state[-1][:, OWN * c : OWN * (c + 1)]


def on_device(noise, plan, slides, w_in, w_mod, w_qkv, qk_gain, w_o, w_out):
    slabs, count = lax.axis_size("slab"), lax.axis_size("seq")
    tokens = count * OWN
    half = FREQ // 2
    freq = np.exp(-math.log(10000.0) * np.arange(half) / half).astype(np.float32)[None]
    smem = pl.BlockSpec(memory_space=pltpu.SMEM)
    vmem = pl.BlockSpec(memory_space=pltpu.VMEM)
    far = pl.BlockSpec(memory_space=pl.ANY)
    block = (PATCH, LANES)

    def sems(n):
        return [pltpu.SemaphoreType.DMA((n,)), pltpu.SemaphoreType.DMA((n,))]

    return pl.pallas_call(
        window_kernel,
        in_specs=[smem, smem, vmem] + [far] * 7,
        out_specs=[vmem, vmem],
        out_shape=[
            jax.ShapeDtypeStruct((STEPS_DEV, CLIPS, PATCH, OWN), f32),
            jax.ShapeDtypeStruct((CLIPS, PATCH, OWN), f32),
        ],
        scratch_shapes=[
            pltpu.VMEM((CLIPS, PATCH, OWN), f32),
            pltpu.VMEM((PATCH, WIDTH), bf16),
            pltpu.VMEM((FREQ, 2 * WIDTH), bf16),
            pltpu.VMEM((WIDTH, WIDTH), bf16),
            pltpu.VMEM((WIDTH, WIDTH), bf16),
            pltpu.VMEM((WIDTH, WIDTH), bf16),
            pltpu.VMEM((2, WIDTH), f32),
            pltpu.VMEM((WIDTH, WIDTH), bf16),
            pltpu.VMEM((WIDTH, PATCH), bf16),
            pltpu.SemaphoreType.DMA((9,)),
            pltpu.VMEM((2 * COMBOS * FE, WIDTH), bf16),
            pltpu.VMEM((COMBOS, FE, 3 * WIDTH), f32),
            pltpu.VMEM((3 * PATCH, PATCH), bf16),
            pltpu.VMEM((COMBOS, HEADS * LANES, LANES), bf16),
            pltpu.VMEM((COMBOS, HEADS * FE, LANES), bf16),
            pltpu.VMEM((COMBOS, HEADS * FE, LANES), bf16),
            pltpu.VMEM((COMBOS, HEADS * 32, WIDTH), bf16),
            pltpu.VMEM((PATCH, WIDTH), bf16),
            pltpu.VMEM(block, f32),
            pltpu.VMEM((1,) + block, bf16),
            pltpu.VMEM((STEPS_DEV,) + block, bf16),
            pltpu.VMEM((count, 1) + block, bf16),
            pltpu.VMEM((count, STEPS_DEV) + block, bf16),
            pltpu.VMEM((STEPS_DEV,) + block, f32),
            pltpu.VMEM((STEPS_DEV,) + block, f32),
            pltpu.VMEM((slabs, STEPS_DEV) + block, f32),
            pltpu.VMEM((slabs, STEPS_DEV) + block, f32),
            *sems(count), *sems(slabs), *sems(count), *sems(slabs),
            pltpu.VMEM((CLIPS, PATCH, tokens), f32),
            pltpu.VMEM((CLIPS * STEPS_DEV, LANES, tokens), bf16),
            pltpu.VMEM((CLIPS * STEPS_DEV, GROUPS, 8, tokens), f32),
            pltpu.VMEM((CLIPS * STEPS_DEV, HEADS // HB, ROWS, LANES), bf16),
            pltpu.VMEM((ROWS, tokens), f32),
            pltpu.VMEM((ROWS, tokens), f32),
            pltpu.VMEM((ROWS, tokens), bf16),
            pltpu.VMEM((ROWS, tokens), bf16),
            pltpu.VMEM((CLIPS * STEPS_DEV, GROUPS, OWN, LANES), bf16),
        ],
        compiler_params=pltpu.CompilerParams(
            collective_id=1, has_side_effects=True, vmem_limit_bytes=56 << 20
        ),
    )(plan, slides, freq, noise, w_in, w_mod, w_qkv, qk_gain, w_o, w_out)


def solution(mesh):
    return jax.shard_map(
        on_device,
        mesh=mesh,
        in_specs=(P(None, None, "seq"), P(), P(), P(), P(), P(), P(), P(), P()),
        out_specs=(P("slab", None, None, "seq"), P(None, None, "seq")),
        check_vma=False,
    )
```

time: 515 us -> 79.5 us (0.15); the launches traced: 505 us -> 79.2 us
  waiting for transfers between devices: 141 us -> 0 us
  matrix products: 118 us -> 0 us
  blocking collectives: 108 us -> 0 us
  Pallas kernels: 0 us -> 74.2 us
  local copies, waits for them, and re-layouts: 71.4 us -> 4.35 us
  starting transfers between devices: 32.2 us -> 0 us
  other arithmetic: 26.6 us -> 0 us
  between operations: 6.25 us -> 0.64 us
    all_to_all x4 -> x0, waiting for transfers between devices: 141 us -> none  [the longest x2 96.8 us: on_device(): lax.all_to_all(packed, 'seq', split_axis=1, concat_axis=2, tiled=True)]
    pallas_call x0 -> x1, Pallas kernels: none -> 74.2 us  [on_device(): pl.pallas_call(window_kernel, in_specs=[smem, smem, vmem] + [far] * 7, ou...]
    all_gather x4 -> x0, blocking collectives: 65.2 us -> none  [the longest x2 32.6 us: on_device(): gathered = lax.all_gather(states, 'slab', axis=0, tiled=True)]
    dot_general x18 -> x0, matrix products: 61.8 us -> none  [the longest x8 39.3 us: one_block(): jnp.einsum('ipqk,ipkh->ipqh', weights_bf, value_part, preferred_element_t...]
    sub x8 -> x0, matrix products: 56.6 us -> none  [one_block(): lifted = jnp.exp(scores - row_max)]
    psum x2 -> x0, blocking collectives: 43 us -> none  [on_device(): drift_sum = lax.psum(own_sum, 'slab')]
    all_to_all x4 -> x0, starting transfers between devices: 32.2 us -> none  [the longest x2 18.1 us: on_device(): lax.all_to_all(packed, 'seq', split_axis=1, concat_axis=2, tiled=True)]
    reshape x12 -> x0, local copies, waits for them, and re-layouts: 31.1 us -> none  [the longest x2 7.64 us: project_in(): joined[..., :model_width].reshape(split_shape)]
  transfers between devices with their start and end apart: 4 -> 0, of which waited for: 4 -> 0; matrix products, arithmetic and copies ran while one was open for 0% -> 0% of each run, Pallas kernels for 0% -> 0%
where the time goes in v2:
time: 79.5 us; the launch traced here: 79.2 us
  Pallas kernels  74.2 us (93%)
  local copies, waits for them, and re-layouts  4.35 us (5%)
    pallas_call x1, Pallas kernels, on_device(): pl.pallas_call(window_kernel, in_specs=[smem, smem, vmem] + [far] * 7, ou...  74.2 us
    unnamed x3, local copies, waits for them, and re-layouts  4.35 us

profile of v2, /device:TPU:1, one launch (start us, length us, event | category | flops | bytes accessed | tf_op | source)
XLA Modules:
  0.0 79.2 jit_solution(10983992213321390407)
XLA Ops:
  0.6 1.6 %copy.12.w_out_hbm = bf16[1152,16]{1,0:T(8,128)(2,1)} copy(bf16[1152,16]{0,1:T(8,128)(2,1)} %param.18) | data formatting | bytes 73728 | tf_op args[8]
  2.3 74.2 %shard_map.113 = (f32[2,2,16,64]{3,2,1,0:T(8,128)}, f32[2,16,64]{2,1,0:T(8,128)}) custom-call(s32[32]{0:T(128)} %plan_ref.1, s32[2]{0:T(128)} %slides_ref.1, f32[1,128]{1,0:T(1,128)} %constant.2.clone.freq_ref, f32[2,16,64]{2,1,0:T(8,128)} %noise_ref.1, bf16[16,1152]{1,0:T(8,128)(2,1)} %w_in_hbm.1, bf16[256,2304]{1,0:T(8,128)(2,1)} %w_mod_hbm.1, ...), custom_call_target="tpu_custom_call" | custom-call | tf_op jit(solution)/shard_map/pallas_call | solution.py:440
  76.5 1.4 %copy.15 = f32[2,2,16,64]{3,2,1,0:T(8,128)} copy(f32[2,2,16,64]{3,2,1,0:T(8,128)} %get-tuple-element.4) | data formatting | bytes 32768
  77.8 1.3 %copy.16 = f32[2,16,64]{2,1,0:T(8,128)} copy(f32[2,16,64]{2,1,0:T(8,128)} %get-tuple-element.5) | data formatting | bytes 16384
